TPU v7x, 256 devices: a whole 4x4x8 slice. The times are simulated.
256 devices in a mesh: gx: 16 (over z, core), gy: 8 (over x, y_lo), seq: 2 (over y_hi).
Axes of the slice: x: 4, y: 4 (y_hi: 2, y_lo: 2; y = y_hi * 2 + y_lo), z: 8, core: 2. Of those that a mesh axis runs over, the one named last changes fastest.
Arguments:
- queries: bfloat16 [32, 64, 16, 1024], P('gx', 'gy', 'seq'), may hold values from -6 to 6
- keys: bfloat16 [2048, 1024], P(('gx', 'gy', 'seq')), may hold values from -8 to 8
- values: bfloat16 [2048, 1024], P(('gx', 'gy', 'seq')), may hold values from -6 to 6
- w_out: bfloat16 [1024, 256], replicated, may hold values from -0.1875 to 0.1875
- conv_first: bfloat16 [3, 3, 3, 256, 128], replicated, may hold values from -0.078125 to 0.078125
- conv_second: bfloat16 [3, 3, 3, 128, 128], replicated, may hold values from -0.109375 to 0.109375
Outputs:
- decoded: bfloat16 [64, 128, 32, 128], P('gx', 'gy', 'seq')
All inputs are finite; a program needn't handle non-finite values.
Results may differ from a plain program's by a relative error of at most 0.02.
Values may be sent and summed in bfloat16 or wider, within the bound.
No kernel may reach another device: no remote copies, remote signals or barrier semaphores. Data moves between devices by JAX's collectives and lax.ppermute only.
A program may use at most 64 MiB of HBM per device.

v0:
```python
import jax
import jax.numpy as jnp
from jax import lax
from jax.sharding import PartitionSpec as P

H = 8


def with_halo(cells, sides, width):
    for axis, dim in sides:
        count = lax.axis_size(axis)
        ends = count - 1
        head = lax.slice_in_dim(cells, 0, width, axis=dim)
        tail = lax.slice_in_dim(cells, cells.shape[dim] - width, cells.shape[dim], axis=dim)
        cells = jnp.concatenate(
            [
                lax.ppermute(tail, axis, [(i, (i + 1) % count) for i in range(ends)]),
                cells,
                lax.ppermute(head, axis, [((i + 1) % count, i) for i in range(ends)]),
            ],
            axis=dim,
        )
    return cells


def conv_layer(padded, weight, size_x, size_y, size_z):
    cin = weight.shape[3]
    cout = weight.shape[4]
    total = jnp.zeros((size_x * size_y * size_z, cout), jnp.float32)
    for a in range(3):
        for b in range(3):
            stacked = jnp.concatenate(
                [padded[a : a + size_x, b : b + size_y, c : c + size_z] for c in range(3)], axis=-1
            )
            stacked = stacked.reshape(-1, 3 * cin)
            total = total + jnp.dot(
                stacked, weight[a, b].reshape(3 * cin, cout), preferred_element_type=jnp.float32
            )
    return total.reshape(size_x, size_y, size_z, cout)


def upsample(field):
    return jnp.repeat(jnp.repeat(jnp.repeat(field, 2, axis=0), 2, axis=1), 2, axis=2)


def head_scores(rows, key_rows, head, head_size):
    query_part = rows[:, head * head_size : (head + 1) * head_size]
    key_part = key_rows[:, head * head_size : (head + 1) * head_size]
    scores = lax.dot_general(
        query_part, key_part, (((1,), (1,)), ((), ())), preferred_element_type=jnp.float32
    )
    return scores * head_size ** (-0.5)


def full_attention(rows, key_rows, value_rows, heads, head_size):
    outputs = []
    for head in range(heads):
        scores = head_scores(rows, key_rows, head, head_size)
        top = jnp.max(scores, axis=1, keepdims=True)
        weights = jnp.exp(scores - top).astype(jnp.bfloat16)
        total = jnp.sum(weights.astype(jnp.float32), axis=1, keepdims=True)
        summed = jnp.dot(
            weights,
            value_rows[:, head * head_size : (head + 1) * head_size],
            preferred_element_type=jnp.float32,
        )
        outputs.append(summed / total)
    return jnp.concatenate(outputs, axis=1).astype(jnp.bfloat16)


def body(queries, keys, values, w_out, conv_first, conv_second):
    size_x, size_y, size_z, width = queries.shape
    heads = H
    head_size = width // heads
    rows = queries.reshape(-1, width)
    key_rows, value_rows = (
        lax.all_gather(keys, ("gx", "gy", "seq"), axis=0, tiled=True),
        lax.all_gather(values, ("gx", "gy", "seq"), axis=0, tiled=True),
    )
    attended = full_attention(rows, key_rows, value_rows, heads, head_size)
    projected = jnp.dot(attended, w_out, preferred_element_type=jnp.float32)
    normed = projected * lax.rsqrt(jnp.mean(projected * projected, axis=-1, keepdims=True) + 1e-06)
    normed = normed.astype(jnp.bfloat16).reshape(size_x, size_y, size_z, w_out.shape[1])
    padded = with_halo(normed, (("gx", 0), ("gy", 1), ("seq", 2)), 1)
    first = conv_layer(padded, conv_first, size_x, size_y, size_z)
    hidden = jax.nn.silu(first).astype(jnp.bfloat16)
    upsampled = upsample(hidden)
    padded_up = with_halo(upsampled, (("gx", 0), ("gy", 1), ("seq", 2)), 1)
    second = conv_layer(padded_up, conv_second, 2 * size_x, 2 * size_y, 2 * size_z)
    return second.astype(jnp.bfloat16)


def solution(mesh):
    in_specs = (
        P("gx", "gy", "seq", None),
        P(("gx", "gy", "seq"), None),
        P(("gx", "gy", "seq"), None),
        P(),
        P(),
        P(),
    )
    out_specs = P("gx", "gy", "seq", None)
    return jax.shard_map(body, mesh=mesh, in_specs=in_specs, out_specs=out_specs, check_vma=False)
```

profile of v0, /device:TPU:97, one launch (start us, length us, event | category | flops | bytes accessed | tf_op | source)
XLA Modules:
  0.0 1512.3 jit_solution(7745640340206660496)
XLA Ops:
  6.5 0.7 all-gather.3.cloned.1.call-update
  8.0 712.1 %all-gather.3.cloned.1.call-done = bf16[2048,1024]{1,0:T(8,128)(2,1)} async-done(((bf16[8,1024]{1,0:T(8,128)(2,1)}), bf16[2048,1024]{1,0:T(8,128)(2,1)}) %all-gather.3.cloned.1.call-update) | async-done | bytes 4194320 | tf_op jit(solution)/shard_map/all_gather | solution.py:77
  720.1 1.6 fusion.71
  722.0 1.4 fusion.72
  728.3 700.2 %all-gather.5.cloned.1.call-done = bf16[2048,1024]{1,0:T(8,128)(2,1)} async-done(((bf16[8,1024]{1,0:T(8,128)(2,1)}), bf16[2048,1024]{1,0:T(8,128)(2,1)}) %all-gather.5.cloned.1.call-update) | async-done | bytes 4194320 | tf_op jit(solution)/shard_map/all_gather | solution.py:78
  1428.5 1.5 fusion.2
  1430.1 1.5 fusion.4
  1431.6 1.5 fusion.6
  1433.2 1.5 fusion.8
  1434.7 1.5 fusion.10
  1436.2 1.4 fusion.12
  1437.7 1.4 fusion.14
  1439.1 1.6 fusion.16
  1441.1 4.5 collective-permute-start
  1445.6 2.5 collective-permute-start.1
  1448.1 4.0 collective-permute-done.1
  1452.1 1.3 collective-permute-start.2
  1453.4 1.3 collective-permute-start.3
  1454.9 5.2 collective-permute-done.3
  1460.1 1.3 collective-permute-start.4
  1461.4 1.3 collective-permute-start.5
  1462.8 4.9 collective-permute-done.5
  1470.1 4.2 collective-permute-start.6
  1474.4 1.9 collective-permute-start.7
  1476.3 4.9 collective-permute-done.7
  1481.4 4.5 collective-permute-start.8
  1485.9 1.3 collective-permute-start.9
  1487.3 3.2 collective-permute-done.9
  1490.8 1.9 collective-permute-start.10
  1492.8 1.5 collective-permute-start.11
  1494.4 4.8 collective-permute-done.11
  1504.4 1.1 fusion
  (117 shorter events, 14.7 us)
Async XLA Ops:
  6.5 1434.1 %copy-start = (bf16[1024,256]{1,0:T(8,128)(2,1)S(1)}, bf16[1024,256]{1,0:T(8,128)(2,1)}, u32[]{:S(2)}) copy-start(bf16[1024,256]{1,0:T(8,128)(2,1)} %param.9) | copy-start | bytes 1572868
  6.5 715.5 %copy-start.16 = (bf16[2,8,8,1024]{3,2,1,0:T(8,128)(2,1)S(1)}, bf16[2,8,8,1024]{3,2,1,0:T(8,128)(2,1)}, u32[]{:S(2)}) copy-start(bf16[2,8,8,1024]{3,2,1,0:T(8,128)(2,1)} %param.6) | copy-start | bytes 786436
  6.5 713.6 %all-gather.3.cloned.1.call-start = ((), (), s32[]{:S(2)}) async-start(), calls=%async_computation | async-start | bytes 4210688 | tf_op jit(solution)/shard_map/all_gather | solution.py:77
  7.3 1421.3 %all-gather.5.cloned.1.call-start = ((), (), s32[]{:S(2)}) async-start(), calls=%async_computation.1 | async-start | bytes 4210688 | tf_op jit(solution)/shard_map/all_gather | solution.py:78
  720.1 3.6 copy-start.1
  723.4 1.1 copy-start.2
  724.2 1.1 copy-start.4
  724.9 1.0 copy-start.6
  725.6 1.0 copy-start.8
  726.4 1.0 copy-start.10
  727.1 1.0 copy-start.12
  1428.5 1.6 copy-start.3
  1428.5 3.1 copy-start.5
  1430.1 3.1 copy-start.7
  1431.6 3.1 copy-start.9
  1433.2 3.1 copy-start.11
  1434.7 3.0 copy-start.13
  1439.1 15.6 %copy-start.14 = (bf16[3,3,3,256,128]{4,3,2,1,0:T(8,128)(2,1)S(1)}, bf16[3,3,3,256,128]{4,3,2,1,0:T(8,128)(2,1)}, u32[]{:S(2)}) copy-start(bf16[3,3,3,256,128]{4,3,2,1,0:T(8,128)(2,1)} %param.10) | copy-start | bytes 5308420
  1441.1 7.0 collective-permute-start
  1445.6 6.4 collective-permute-start.1
  1452.1 2.8 collective-permute-start.2
  1453.4 6.7 collective-permute-start.3
  1460.1 2.7 collective-permute-start.4
  1461.4 6.3 collective-permute-start.5
  1469.4 17.9 %copy-start.15 = (bf16[3,3,3,128,128]{4,3,2,1,0:T(8,128)(2,1)S(1)}, bf16[3,3,3,128,128]{4,3,2,1,0:T(8,128)(2,1)}, u32[]{:S(2)}) copy-start(bf16[3,3,3,128,128]{4,3,2,1,0:T(8,128)(2,1)} %param.11) | copy-start | bytes 2654212
  1470.1 6.2 collective-permute-start.6
  1474.4 6.8 collective-permute-start.7
  1481.4 5.9 collective-permute-start.8
  1485.9 4.6 collective-permute-start.9
  1490.8 3.6 collective-permute-start.10
  1492.8 6.4 collective-permute-start.11
Sparse Core Ops, SparseCore 0:
  9.2 710.8 all-gather.2
  722.0 706.4 all-gather.4
where the time goes:
time: 1510 us
  waiting for transfers between devices  1440 us (95%)
  starting transfers between devices  27.6 us (2%)
  matrix products  23.6 us (2%)
    all_gather x1, waiting for transfers between devices, body(): lax.all_gather(keys, ('gx', 'gy', 'seq'), axis=0, tiled=True)  712 us
    all_gather x1, waiting for transfers between devices, body(): lax.all_gather(values, ('gx', 'gy', 'seq'), axis=0, tiled=True)  700 us
  transfers between devices with their start and end apart: 14, of which 8 were waited for; matrix products, arithmetic and copies ran while one was open for 1% of the time, Pallas kernels for 0%

commit v1 on v0

--- a/solution.py
+++ b/solution.py
@@ -4,6 +4,13 @@
 from jax.sharding import PartitionSpec as P
 
 H = 8
+
+
+def exchange_gather(x, mesh_axis, d):
+    devices = lax.axis_size(mesh_axis)
+    blocks = jnp.stack([x for _ in range(devices)])
+    blocks = lax.all_to_all(blocks, mesh_axis, split_axis=0, concat_axis=0)
+    return jnp.concatenate(blocks, axis=d)
 
 
 def with_halo(cells, sides, width):
@@ -74,7 +81,7 @@
     head_size = width // heads
     rows = queries.reshape(-1, width)
     key_rows, value_rows = (
-        lax.all_gather(keys, ("gx", "gy", "seq"), axis=0, tiled=True),
+        exchange_gather(keys, ("gx", "gy", "seq"), 0),
         lax.all_gather(values, ("gx", "gy", "seq"), axis=0, tiled=True),
     )
     attended = full_attention(rows, key_rows, value_rows, heads, head_size)

time: 1510 us -> 837 us (0.55)
  waiting for transfers between devices: 1440 us -> 741 us
    all_gather x1 -> x0, waiting for transfers between devices: 712 us -> none  [body(): lax.all_gather(keys, ('gx', 'gy', 'seq'), axis=0, tiled=True)]
    all_to_all x0 -> x1, waiting for transfers between devices: none -> 93 us  [exchange_gather(): blocks = lax.all_to_all(blocks, mesh_axis, split_axis=0, concat_axis=0)]
    all_gather x1, waiting for transfers between devices: 700 us -> 620 us  [body(): lax.all_gather(values, ('gx', 'gy', 'seq'), axis=0, tiled=True)]
    all_to_all x0 -> x1, starting transfers between devices: none -> 15.3 us  [exchange_gather(): blocks = lax.all_to_all(blocks, mesh_axis, split_axis=0, concat_axis=0)]
  transfers between devices with their start and end apart: 14 -> 14, of which waited for: 8 -> 8; matrix products, arithmetic and copies ran while one was open for 1% -> 2% of each run, Pallas kernels for 0% -> 0%
where the time goes in v1:
time: 837 us; the launch traced here: 836 us
  waiting for transfers between devices  741 us (89%)
  starting transfers between devices  41.8 us (5%)
  matrix products  29.9 us (4%)
  between operations  14.2 us (2%)
    all_gather x1, waiting for transfers between devices, body(): lax.all_gather(values, ('gx', 'gy', 'seq'), axis=0, tiled=True)  620 us
    all_to_all x1, waiting for transfers between devices, exchange_gather(): blocks = lax.all_to_all(blocks, mesh_axis, split_axis=0, concat_axis=0)  93 us
    ppermute x6, waiting for transfers between devices, with_halo(): lax.ppermute(head, axis, [((i + 1) % count, i) for i in range(ends)])  27.1 us
  transfers between devices with their start and end apart: 14, of which 8 were waited for; matrix products, arithmetic and copies ran while one was open for 2% of the time, Pallas kernels for 0%

profile of v1, /device:TPU:97, one launch (start us, length us, event | category | flops | bytes accessed | tf_op | source)
XLA Modules:
  0.0 836.5 jit_solution(18147735027182744413)
XLA Ops:
  6.5 3.3 stack.2
  9.8 15.3 %all-to-all-start = ((bf16[256,8,1024]{2,1,0:T(8,128)(2,1)}), bf16[256,8,1024]{2,1,0:T(8,128)(2,1)}, u32[]{:S(2)}, u32[]{:S(2)}) async-start(bf16[256,8,1024]{2,1,0:T(8,128)(2,1)} %stack.2), calls=%async_computation | async-start | bytes 8388608 | tf_op jit(solution)/shard_map/all_to_all | solution.py:12
  25.9 93.0 %all-to-all-done = bf16[256,8,1024]{2,1,0:T(8,128)(2,1)} async-done(((bf16[256,8,1024]{2,1,0:T(8,128)(2,1)}), bf16[256,8,1024]{2,1,0:T(8,128)(2,1)}, u32[]{:S(2)}, u32[]{:S(2)}) %all-to-all-start) | async-done | bytes 4194336 | tf_op jit(solution)/shard_map/all_to_all | solution.py:12
  120.6 1.4 fusion.72
  122.3 1.5 fusion.73
  124.1 1.5 fusion.74
  125.9 1.5 fusion.75
  127.7 1.5 fusion.76
  129.5 1.5 fusion.77
  131.3 1.5 fusion.78
  133.1 620.4 %all-gather.2.cloned.1.call-done = bf16[2048,1024]{1,0:T(8,128)(2,1)} async-done(((bf16[8,1024]{1,0:T(8,128)(2,1)}), bf16[2048,1024]{1,0:T(8,128)(2,1)}) %all-gather.2.cloned.1.call-update) | async-done | bytes 4194320 | tf_op jit(solution)/shard_map/all_gather | solution.py:85
  753.5 1.5 fusion.2
  755.1 1.5 fusion.4
  756.6 1.5 fusion.6
  758.2 1.5 fusion.8
  759.7 1.5 fusion.10
  761.2 1.4 fusion.12
  762.7 1.4 fusion.14
  764.1 1.6 fusion.16
  766.1 3.4 collective-permute-start
  769.5 2.5 collective-permute-start.1
  772.0 4.0 collective-permute-done.1
  778.8 5.5 collective-permute-done.3
  787.0 4.9 collective-permute-done.5
  794.3 4.2 collective-permute-start.6
  798.6 1.9 collective-permute-start.7
  800.5 4.9 collective-permute-done.7
  805.6 4.5 collective-permute-start.8
  811.5 3.2 collective-permute-done.9
  815.0 1.9 collective-permute-start.10
  817.0 1.5 collective-permute-start.11
  818.6 4.8 collective-permute-done.11
  (115 shorter events, 20.9 us)
Async XLA Ops:
  6.5 759.1 %copy-start = (bf16[1024,256]{1,0:T(8,128)(2,1)S(1)}, bf16[1024,256]{1,0:T(8,128)(2,1)}, u32[]{:S(2)}) copy-start(bf16[1024,256]{1,0:T(8,128)(2,1)} %param.9) | copy-start | bytes 1572868
  9.8 109.0 %copy-start.15 = (bf16[2,8,8,1024]{3,2,1,0:T(8,128)(2,1)S(1)}, bf16[2,8,8,1024]{3,2,1,0:T(8,128)(2,1)}, u32[]{:S(2)}) copy-start(bf16[2,8,8,1024]{3,2,1,0:T(8,128)(2,1)} %param.6) | copy-start | bytes 786436
  9.8 109.0 %all-to-all-start = ((bf16[256,8,1024]{2,1,0:T(8,128)(2,1)}), bf16[256,8,1024]{2,1,0:T(8,128)(2,1)}, u32[]{:S(2)}, u32[]{:S(2)}) async-start(bf16[256,8,1024]{2,1,0:T(8,128)(2,1)} %stack.2), calls=%async_computation | async-start | bytes 8388608 | tf_op jit(solution)/shard_map/all_to_all | solution.py:12
  25.1 728.4 %all-gather.2.cloned.1.call-start = ((), (), s32[]{:S(2)}) async-start(), calls=%async_computation.1 | async-start | bytes 4210688 | tf_op jit(solution)/shard_map/all_gather | solution.py:85
  122.0 2.1 copy-start.1
  123.8 2.1 copy-start.3
  125.6 2.1 copy-start.5
  127.4 2.1 copy-start.7
  129.2 2.1 copy-start.9
  131.0 1.8 copy-start.11
  753.5 1.6 copy-start.2
  753.5 3.1 copy-start.4
  755.1 3.1 copy-start.6
  756.6 3.1 copy-start.8
  758.2 3.1 copy-start.10
  759.7 3.0 copy-start.12
  764.1 14.5 %copy-start.13 = (bf16[3,3,3,256,128]{4,3,2,1,0:T(8,128)(2,1)S(1)}, bf16[3,3,3,256,128]{4,3,2,1,0:T(8,128)(2,1)}, u32[]{:S(2)}) copy-start(bf16[3,3,3,256,128]{4,3,2,1,0:T(8,128)(2,1)} %param.10) | copy-start | bytes 5308420
  766.1 5.9 collective-permute-start
  769.5 6.4 collective-permute-start.1
  776.0 2.8 collective-permute-start.2
  777.3 7.0 collective-permute-start.3
  784.3 2.7 collective-permute-start.4
  785.6 6.3 collective-permute-start.5
  793.6 17.9 %copy-start.14 = (bf16[3,3,3,128,128]{4,3,2,1,0:T(8,128)(2,1)S(1)}, bf16[3,3,3,128,128]{4,3,2,1,0:T(8,128)(2,1)}, u32[]{:S(2)}) copy-start(bf16[3,3,3,128,128]{4,3,2,1,0:T(8,128)(2,1)} %param.11) | copy-start | bytes 2654212
  794.3 6.2 collective-permute-start.6
  798.6 6.8 collective-permute-start.7
  805.6 5.9 collective-permute-start.8
  810.1 4.6 collective-permute-start.9
  815.0 3.6 collective-permute-start.10
  817.0 6.4 collective-permute-start.11
Sparse Core Ops, SparseCore 0:
  27.9 725.6 all-gather.1
